TPU v7x, 32 devices: a whole 2x2x4 slice. The times are simulated.
32 devices in a mesh: groups: 2 (over x), seq: 16 (over z, y, core).
Axes of the slice: x: 2, y: 2, z: 4, core: 2. Of those that a mesh axis runs over, the one named last changes fastest.
Arguments:
- inputs: bfloat16 [16384, 768], P(('groups', 'seq')), parts along dimension 0, may hold values from -6 to 6
- gates: bfloat16 [16384, 768], P(('groups', 'seq')), parts along dimension 0, may hold values from -6 to 6
- cotangent: bfloat16 [16384, 768], P(('groups', 'seq')), parts along dimension 0, may hold values from -6 to 6
- first_factor: bfloat16 [16, 512, 512], P('seq'), may hold values from -0.25 to 0.25
- second_factor: bfloat16 [512, 16, 16], P('seq'), may hold values from -1.5 to 1.5
- channel_gain: float32 [768], replicated, may hold values from 0.1 to 1.9
Outputs:
- layer_output: bfloat16 [16384, 768], P(('groups', 'seq')), parts along dimension 0
- grad_inputs: bfloat16 [16384, 768], P(('groups', 'seq')), parts along dimension 0
- grad_gates: bfloat16 [16384, 768], P(('groups', 'seq')), parts along dimension 0
- grad_first: bfloat16 [32, 512, 512], P(('groups', 'seq')), parts along dimension 0
- grad_second: bfloat16 [1024, 16, 16], P(('groups', 'seq')), parts along dimension 0
- gain_grad: float32 [1536], P('groups'), parts along dimension 0
There are 2 independent parts, one for each index of `groups`. A program takes and returns all parts, laid end to end along the dimension named above; an argument that names none is the same for every part. Nothing has to cross between parts.
All inputs are finite; a program needn't handle non-finite values.
Results may differ from a plain program's by a relative error of at most 0.0085.
Values may be sent and summed in bfloat16 or wider, within the bound.
A program may use at most 64 MiB of HBM per device.

v0:
```python
import math
import jax
import jax.numpy as jnp
from jax import lax
from jax.sharding import PartitionSpec as P


def lower_mask(extent):
    row_ids = lax.broadcasted_iota(jnp.int32, (extent, extent), 0)
    col_ids = lax.broadcasted_iota(jnp.int32, (extent, extent), 1)
    return col_ids <= row_ids


def on_device(inputs, gates, cotangent, first_factor, second_factor, channel_gain):
    block_count = first_factor.shape[0]
    block_size = first_factor.shape[1]
    channels = inputs.shape[1]
    block_total = second_factor.shape[1]
    rows3 = inputs.reshape(block_count, block_size, channels)
    gates3 = gates.reshape(block_count, block_size, channels)
    upstream3 = cotangent.reshape(block_count, block_size, channels)
    mask_first = lower_mask(block_size)
    mask_second = lower_mask(block_total)
    first_masked = jnp.where(mask_first[None], first_factor, jnp.zeros((), first_factor.dtype))
    second_masked = jnp.where(mask_second[None], second_factor, jnp.zeros((), second_factor.dtype))
    norm_factor = 1.0 / math.sqrt(inputs.shape[0] * lax.axis_size("seq"))
    gates_cols, upstream_cols = (
        lax.all_to_all(gates3, "seq", split_axis=1, concat_axis=0, tiled=True),
        lax.all_to_all(upstream3, "seq", split_axis=1, concat_axis=0, tiled=True),
    )
    first_mixed = jnp.einsum(
        "kab,kbc->kac", first_masked, rows3, preferred_element_type=jnp.float32
    ).astype(jnp.bfloat16)
    columns = lax.all_to_all(first_mixed, "seq", split_axis=1, concat_axis=0, tiled=True)
    second_cols = jnp.einsum(
        "jab,bjc->ajc", second_masked, columns, preferred_element_type=jnp.float32
    ).astype(jnp.bfloat16)
    hidden_values = second_cols.astype(jnp.float32)
    gate_values = gates_cols.astype(jnp.float32)
    upstream_values = upstream_cols.astype(jnp.float32)
    output_cols = (gate_values * channel_gain * hidden_values).astype(jnp.bfloat16)
    hidden_cols = (upstream_values * gate_values * channel_gain).astype(jnp.bfloat16)
    grad_gate_cols = (upstream_values * channel_gain * hidden_values).astype(jnp.bfloat16)
    partial_gain = jnp.sum(upstream_values * gate_values * hidden_values, axis=(0, 1))
    grad_pairs = jnp.einsum(
        "ajc,bjc->jab", hidden_cols, columns, preferred_element_type=jnp.float32
    )
    grad_sec = jnp.where(mask_second[None], grad_pairs, jnp.zeros((), jnp.float32)).astype(
        jnp.bfloat16
    )
    back_cols = jnp.einsum(
        "jab,ajc->bjc", second_masked, hidden_cols, preferred_element_type=jnp.float32
    ).astype(jnp.bfloat16)
    back_rows, output_rows, grad_gate_rows = (
        lax.all_to_all(back_cols, "seq", split_axis=0, concat_axis=1, tiled=True),
        lax.all_to_all(output_cols, "seq", split_axis=0, concat_axis=1, tiled=True),
        lax.all_to_all(grad_gate_cols, "seq", split_axis=0, concat_axis=1, tiled=True),
    )
    gain_grad = lax.psum(partial_gain, "seq") * norm_factor
    grad_pairs_first = jnp.einsum(
        "kac,kbc->kab", back_rows, rows3, preferred_element_type=jnp.float32
    )
    grad_first = jnp.where(mask_first[None], grad_pairs_first, jnp.zeros((), jnp.float32)).astype(
        jnp.bfloat16
    )
    grad_in = jnp.einsum(
        "kab,kac->kbc", first_masked, back_rows, preferred_element_type=jnp.float32
    ).astype(jnp.bfloat16)
    token_rows = inputs.shape[0]
    return (
        output_rows.reshape(token_rows, channels),
        grad_in.reshape(token_rows, channels),
        grad_gate_rows.reshape(token_rows, channels),
        grad_first,
        grad_sec,
        gain_grad,
    )


def solution(mesh):
    placed = (
        P(("groups", "seq"), None),
        P(("groups", "seq"), None),
        P(("groups", "seq"), None),
        P("seq", None, None),
        P("seq", None, None),
        P(),
    )
    return jax.shard_map(
        on_device,
        mesh=mesh,
        in_specs=placed,
        out_specs=(
            P(("groups", "seq"), None),
            P(("groups", "seq"), None),
            P(("groups", "seq"), None),
            P(("groups", "seq"), None, None),
            P(("groups", "seq"), None, None),
            P("groups"),
        ),
        check_vma=False,
    )
```

profile of v0, /device:TPU:0, one launch (start us, length us, event | category | flops | bytes accessed | tf_op | source)
XLA Modules:
  0.0 196.3 jit_solution(10928412952804270693)
XLA Ops:
  0.6 0.0 copy-start
  0.6 1.1 copy-done
  1.8 1.6 fusion.5
  3.4 1.2 copy.83
  4.6 0.5 broadcast.2
  5.1 5.4 %reduce.2 = bf16[512,768]{1,0:T(8,128)(2,1)S(1)} reduce(bf16[512,1,768]{2,1,0:T(2,128)(2,1)S(1)} %bitcast.48, bf16[]{:T(256)} %broadcast.2), dimensions={1}, to_apply=%bitcast.46.reduce_sub_computation | reduce | bytes 1572866
  10.6 1.1 reshape.99
  11.6 0.0 copy-start.4
  11.6 7.6 %all-to-all-start.1 = ((bf16[16,2,12288]{2,1,0:T(2,128)(2,1)}), bf16[16,2,12288]{2,1,0:T(2,128)(2,1)}, u32[]{:S(2)}, u32[]{:S(2)}) async-start(bf16[16,2,12288]{2,1,0:T(2,128)(2,1)} %reshape.99), calls=%async_computation.1 | async-start | bytes 1572864 | tf_op jit(solution)/shard_map/all_to_all | solution.py:34
  19.2 0.0 copy-done.4
  19.2 1.2 copy.84
  20.4 5.4 %reduce = bf16[512,768]{1,0:T(8,128)(2,1)S(1)} reduce(bf16[512,1,768]{2,1,0:T(2,128)(2,1)S(1)} %bitcast.53, bf16[]{:T(256)} %broadcast.2), dimensions={1}, to_apply=%bitcast.47.reduce_sub_computation | reduce | bytes 1572866
  25.9 1.1 reshape.101
  26.9 0.0 copy-start.5
  26.9 11.0 %all-to-all-done.1 = bf16[16,2,12288]{2,1,0:T(2,128)(2,1)} async-done(((bf16[16,2,12288]{2,1,0:T(2,128)(2,1)}), bf16[16,2,12288]{2,1,0:T(2,128)(2,1)}, u32[]{:S(2)}, u32[]{:S(2)}) %all-to-all-start.1) | async-done | bytes 786464 | tf_op jit(solution)/shard_map/all_to_all | solution.py:34
  38.0 5.5 %all-to-all-start = ((bf16[16,2,12288]{2,1,0:T(2,128)(2,1)}), bf16[16,2,12288]{2,1,0:T(2,128)(2,1)}, u32[]{:S(2)}, u32[]{:S(2)}) async-start(bf16[16,2,12288]{2,1,0:T(2,128)(2,1)} %reshape.101), calls=%async_computation | async-start | bytes 1572864 | tf_op jit(solution)/shard_map/all_to_all | solution.py:28
  43.5 0.0 copy-done.5
  43.5 1.2 copy.82
  44.7 5.4 %reduce.1 = bf16[512,768]{1,0:T(8,128)(2,1)S(1)} reduce(bf16[512,1,768]{2,1,0:T(2,128)(2,1)S(1)} %bitcast.49, bf16[]{:T(256)} %broadcast.2), dimensions={1}, to_apply=%bitcast.45.reduce_sub_computation | reduce | bytes 1572866
  50.2 0.0 copy-start.6
  50.2 1.1 reshape.103
  51.2 11.0 %all-to-all-done = bf16[16,2,12288]{2,1,0:T(2,128)(2,1)} async-done(((bf16[16,2,12288]{2,1,0:T(2,128)(2,1)}), bf16[16,2,12288]{2,1,0:T(2,128)(2,1)}, u32[]{:S(2)}, u32[]{:S(2)}) %all-to-all-start) | async-done | bytes 786464 | tf_op jit(solution)/shard_map/all_to_all | solution.py:28
  62.3 5.5 %all-to-all-start.3 = ((bf16[16,2,12288]{2,1,0:T(2,128)(2,1)}), bf16[16,2,12288]{2,1,0:T(2,128)(2,1)S(1)}, u32[]{:S(2)}, u32[]{:S(2)}) async-start(bf16[16,2,12288]{2,1,0:T(2,128)(2,1)} %reshape.103), calls=%async_computation.3 | async-start | bytes 1572864 | tf_op jit(solution)/shard_map/all_to_all | solution.py:29
  67.7 0.0 copy-done.6
  67.8 0.2 copy.46
  67.9 4.4 %reshape.100 = bf16[512,1,768]{2,1,0:T(2,128)(2,1)S(1)} reshape(bf16[16,2,12288]{2,1,0:T(2,128)(2,1)} %all-to-all-done.1) | data formatting | bytes 1572864
  72.3 1.0 copy.60
  73.3 4.4 %reshape.102 = bf16[512,1,768]{2,1,0:T(2,128)(2,1)S(1)} reshape(bf16[16,2,12288]{2,1,0:T(2,128)(2,1)} %all-to-all-done) | data formatting | bytes 1572864
  77.7 0.1 copy.43
  77.8 1.3 convert.3
  79.1 7.3 %all-to-all-done.3 = bf16[16,2,12288]{2,1,0:T(2,128)(2,1)S(1)} async-done(((bf16[16,2,12288]{2,1,0:T(2,128)(2,1)}), bf16[16,2,12288]{2,1,0:T(2,128)(2,1)S(1)}, u32[]{:S(2)}, u32[]{:S(2)}) %all-to-all-start.3) | async-done | bytes 786464 | tf_op jit(solution)/shard_map/all_to_all | solution.py:29
  86.4 0.7 reshape.104
  87.2 0.0 copy-start.7
  87.2 0.1 copy.50
  87.3 0.0 copy-start.1
  87.3 0.0 copy-start.2
  87.4 0.2 convert.4
  87.5 0.4 copy-done.7
  87.9 0.8 copy-done.1
  88.7 0.2 copy-done.2
  88.9 2.4 %fusion.2 = (f32[768]{0:T(1024)S(1)}, bf16[16,32,768]{2,0,1:T(8,128)(2,1)S(1)}, bf16[16,32,768]{2,0,1:T(8,128)(2,1)S(1)}, bf16[16,32,768]{2,0,1:T(8,128)(2,1)S(1)}) fusion(f32[16,32,768]{2,1,0:T(8,128)S(1)} %copy-done.1, f32[16,32,768]{2,1,0:T(8,128)S(1)} %convert.4, f32[768]{0:T(1024)S(1)} %copy-done.7, bf16[16,32,768]{2,1,0:T(8,128)(2,1)S(1)} %bitcast.58, ...), kind=kOutput, calls=%fused_computation.5 | convolution fusion | flops 17702144 | bytes 6314240 | tf_op jit(solution)/shard_map/jab,bjc->ajc/dot_general | solution.py:35
  91.4 0.0 copy-start.3
  91.4 0.9 copy-done.3
  92.3 0.4 fusion.4
  92.7 1.1 copy.54
  93.8 5.5 %all-to-all-start.4 = ((bf16[16,32,768]{2,1,0:T(8,128)(2,1)}), bf16[16,32,768]{2,1,0:T(8,128)(2,1)}, u32[]{:S(2)}, u32[]{:S(2)}) async-start(bf16[16,32,768]{2,1,0:T(8,128)(2,1)} %copy.54), calls=%async_computation.4 | async-start | bytes 1572864 | tf_op jit(solution)/shard_map/all_to_all | solution.py:55
  99.3 1.1 copy.56
  100.5 17.7 %all-to-all-done.4 = bf16[16,32,768]{2,1,0:T(8,128)(2,1)} async-done(((bf16[16,32,768]{2,1,0:T(8,128)(2,1)}), bf16[16,32,768]{2,1,0:T(8,128)(2,1)}, u32[]{:S(2)}, u32[]{:S(2)}) %all-to-all-start.4) | async-done | bytes 786464 | tf_op jit(solution)/shard_map/all_to_all | solution.py:55
  118.1 5.5 %all-to-all-start.5 = ((bf16[16,32,768]{2,1,0:T(8,128)(2,1)}), bf16[16,32,768]{2,1,0:T(8,128)(2,1)S(1)}, u32[]{:S(2)}, u32[]{:S(2)}) async-start(bf16[16,32,768]{2,1,0:T(8,128)(2,1)} %copy.56), calls=%async_computation.5 | async-start | bytes 1572864 | tf_op jit(solution)/shard_map/all_to_all | solution.py:57
  123.6 1.1 copy.48
  124.7 17.6 %all-to-all-done.5 = bf16[16,32,768]{2,1,0:T(8,128)(2,1)S(1)} async-done(((bf16[16,32,768]{2,1,0:T(8,128)(2,1)}), bf16[16,32,768]{2,1,0:T(8,128)(2,1)S(1)}, u32[]{:S(2)}, u32[]{:S(2)}) %all-to-all-start.5) | async-done | bytes 786464 | tf_op jit(solution)/shard_map/all_to_all | solution.py:57
  142.3 5.5 %all-to-all-start.2 = ((bf16[16,32,768]{2,1,0:T(8,128)(2,1)}), bf16[16,32,768]{2,1,0:T(8,128)(2,1)S(1)}, u32[]{:S(2)}, u32[]{:S(2)}) async-start(bf16[16,32,768]{2,1,0:T(8,128)(2,1)} %copy.48), calls=%async_computation.2 | async-start | bytes 1572864 | tf_op jit(solution)/shard_map/all_to_all | solution.py:56
  147.8 1.7 fusion.7
  149.5 0.0 copy-start.8
  149.5 0.8 copy.58
  150.3 38.5 %psum.7 = f32[768]{0:T(1024)S(1)} all-reduce(f32[768]{0:T(1024)S(1)} %get-tuple-element.30), channel_id=1, replica_groups=mesh['groups'=2,'seq'=16] {'seq'}, use_global_device_ids=true, to_apply=%region_1.2 | all-reduce | flops 768 | bytes 6144 | tf_op jit(solution)/shard_map/psum | solution.py:59
  188.8 0.6 broadcast_multiply_fusion
  189.4 2.5 %fusion.6 = bf16[1,512,512]{2,1,0:T(8,128)(2,1)} fusion(bf16[512,768]{1,0:T(8,128)(2,1)} %bitcast.10, bf16[512,768]{1,0:T(8,128)(2,1)S(1)} %copy-done), kind=kOutput, calls=%fused_computation.16 | convolution fusion | flops 403439616 | bytes 2097152 | tf_op jit(solution)/shard_map/kac,kbc->kab/dot_general | solution.py:60
  191.9 0.0 copy-done.8
  191.9 2.6 %convolution_convert_fusion = bf16[512,768]{1,0:T(8,128)(2,1)} fusion(bf16[512,768]{1,0:T(8,128)(2,1)} %bitcast.10, bf16[1,512,512]{2,1,0:T(8,128)(2,1)S(1)} %copy-done.8), kind=kOutput, calls=%fused_computation.8 | convolution fusion | flops 403570688 | bytes 2097152 | tf_op jit(solution)/shard_map/kab,kac->kbc/dot_general | solution.py:66
  194.5 0.0 all-to-all-done.2
  194.5 0.9 copy.87
  195.4 0.9 copy.88
  (1 shorter events, 0.0 us)
Async XLA Ops:
  0.6 1.1 copy-start
  11.6 7.6 %copy-start.4 = (bf16[512,768]{1,0:T(8,128)(2,1)S(1)}, bf16[512,768]{1,0:T(8,128)(2,1)}, u32[]{:S(2)}) copy-start(bf16[512,768]{1,0:T(8,128)(2,1)} %param.7) | copy-start | bytes 2359300
  11.6 26.3 %all-to-all-start.1 = ((bf16[16,2,12288]{2,1,0:T(2,128)(2,1)}), bf16[16,2,12288]{2,1,0:T(2,128)(2,1)}, u32[]{:S(2)}, u32[]{:S(2)}) async-start(bf16[16,2,12288]{2,1,0:T(2,128)(2,1)} %reshape.99), calls=%async_computation.1 | async-start | bytes 1572864 | tf_op jit(solution)/shard_map/all_to_all | solution.py:34
  26.9 16.6 %copy-start.5 = (bf16[512,768]{1,0:T(8,128)(2,1)S(1)}, bf16[512,768]{1,0:T(8,128)(2,1)}, u32[]{:S(2)}) copy-start(bf16[512,768]{1,0:T(8,128)(2,1)} %param.8) | copy-start | bytes 2359300
  38.0 24.3 %all-to-all-start = ((bf16[16,2,12288]{2,1,0:T(2,128)(2,1)}), bf16[16,2,12288]{2,1,0:T(2,128)(2,1)}, u32[]{:S(2)}, u32[]{:S(2)}) async-start(bf16[16,2,12288]{2,1,0:T(2,128)(2,1)} %reshape.101), calls=%async_computation | async-start | bytes 1572864 | tf_op jit(solution)/shard_map/all_to_all | solution.py:28
  50.2 17.6 %copy-start.6 = (bf16[32,16,16]{0,2,1:T(8,128)(2,1)S(1)}, bf16[32,16,16]{0,2,1:T(8,128)(2,1)}, u32[]{:S(2)}) copy-start(bf16[32,16,16]{0,2,1:T(8,128)(2,1)} %param.10) | copy-start | bytes 49156
  62.3 24.2 %all-to-all-start.3 = ((bf16[16,2,12288]{2,1,0:T(2,128)(2,1)}), bf16[16,2,12288]{2,1,0:T(2,128)(2,1)S(1)}, u32[]{:S(2)}, u32[]{:S(2)}) async-start(bf16[16,2,12288]{2,1,0:T(2,128)(2,1)} %reshape.103), calls=%async_computation.3 | async-start | bytes 1572864 | tf_op jit(solution)/shard_map/all_to_all | solution.py:29
  87.2 0.7 copy-start.7
  87.3 1.4 copy-start.1
  87.3 1.6 copy-start.2
  91.4 0.9 copy-start.3
  93.8 24.3 %all-to-all-start.4 = ((bf16[16,32,768]{2,1,0:T(8,128)(2,1)}), bf16[16,32,768]{2,1,0:T(8,128)(2,1)}, u32[]{:S(2)}, u32[]{:S(2)}) async-start(bf16[16,32,768]{2,1,0:T(8,128)(2,1)} %copy.54), calls=%async_computation.4 | async-start | bytes 1572864 | tf_op jit(solution)/shard_map/all_to_all | solution.py:55
  118.1 24.2 %all-to-all-start.5 = ((bf16[16,32,768]{2,1,0:T(8,128)(2,1)}), bf16[16,32,768]{2,1,0:T(8,128)(2,1)S(1)}, u32[]{:S(2)}, u32[]{:S(2)}) async-start(bf16[16,32,768]{2,1,0:T(8,128)(2,1)} %copy.56), calls=%async_computation.5 | async-start | bytes 1572864 | tf_op jit(solution)/shard_map/all_to_all | solution.py:57
  142.3 52.2 %all-to-all-start.2 = ((bf16[16,32,768]{2,1,0:T(8,128)(2,1)}), bf16[16,32,768]{2,1,0:T(8,128)(2,1)S(1)}, u32[]{:S(2)}, u32[]{:S(2)}) async-start(bf16[16,32,768]{2,1,0:T(8,128)(2,1)} %copy.48), calls=%async_computation.2 | async-start | bytes 1572864 | tf_op jit(solution)/shard_map/all_to_all | solution.py:56
  149.5 42.4 %copy-start.8 = (bf16[1,512,512]{2,1,0:T(8,128)(2,1)S(1)}, bf16[1,512,512]{2,1,0:T(8,128)(2,1)}, u32[]{:S(2)}) copy-start(bf16[1,512,512]{2,1,0:T(8,128)(2,1)} %param.9) | copy-start | bytes 1572868
where the time goes:
time: 197 us; the launch traced here: 196 us
  waiting for transfers between devices  64.6 us (33%)
  blocking collectives  38.5 us (20%)
  starting transfers between devices  35.1 us (18%)
  local copies, waits for them, and re-layouts  27.5 us (14%)
  other arithmetic  18.3 us (9%)
  matrix products  11.3 us (6%)
    psum x1, blocking collectives, on_device(): gain_grad = lax.psum(partial_gain, 'seq') * norm_factor  38.5 us
    unnamed x30, local copies, waits for them, and re-layouts  20.3 us
    all_to_all x1, waiting for transfers between devices, on_device(): lax.all_to_all(back_cols, 'seq', split_axis=0, concat_axis=1, tiled=True)  17.7 us
    all_to_all x1, waiting for transfers between devices, on_device(): lax.all_to_all(grad_gate_cols, 'seq', split_axis=0, concat_axis=1, tiled=...  17.6 us
    unnamed x3, other arithmetic  16.3 us
    all_to_all x1, waiting for transfers between devices, on_device(): lax.all_to_all(first_mixed, 'seq', split_axis=1, concat_axis=0, tiled=True)  11 us
    all_to_all x1, waiting for transfers between devices, on_device(): lax.all_to_all(gates3, 'seq', split_axis=1, concat_axis=0, tiled=True)  11 us
    all_to_all x1, starting transfers between devices, on_device(): lax.all_to_all(first_mixed, 'seq', split_axis=1, concat_axis=0, tiled=True)  7.57 us
  transfers between devices with their start and end apart: 6, of which 5 were waited for; matrix products, arithmetic and copies ran while one was open for 19% of the time, Pallas kernels for 0%

commit v1 on v0

--- a/solution.py
+++ b/solution.py
@@ -56,7 +56,7 @@
         lax.all_to_all(output_cols, "seq", split_axis=0, concat_axis=1, tiled=True),
         lax.all_to_all(grad_gate_cols, "seq", split_axis=0, concat_axis=1, tiled=True),
     )
-    gain_grad = lax.psum(partial_gain, "seq") * norm_factor
+    gain_grad = jnp.sum(lax.all_gather(partial_gain, "seq"), axis=0) * norm_factor
     grad_pairs_first = jnp.einsum(
         "kac,kbc->kab", back_rows, rows3, preferred_element_type=jnp.float32
     )

time: 197 us -> 186 us (0.944)
  blocking collectives: 38.5 us -> 26.9 us
    psum x1 -> x0, blocking collectives: 38.5 us -> none  [on_device(): gain_grad = lax.psum(partial_gain, 'seq') * norm_factor]
    all_gather x0 -> x1, blocking collectives: none -> 26.9 us  [on_device(): lax.all_gather(partial_gain, 'seq')]
    unnamed x30 -> x31, local copies, waits for them, and re-layouts: 20.3 us -> 20.3 us
  transfers between devices with their start and end apart: 6 -> 6, of which waited for: 5 -> 5; matrix products, arithmetic and copies ran while one was open for 19% -> 20% of each run, Pallas kernels for 0% -> 0%
where the time goes in v1:
time: 186 us; the launch traced here: 185 us
  waiting for transfers between devices  64.6 us (35%)
  starting transfers between devices  35.1 us (19%)
  local copies, waits for them, and re-layouts  27.5 us (15%)
  blocking collectives  26.9 us (14%)
  other arithmetic  18.4 us (10%)
  matrix products  11.3 us (6%)
    all_gather x1, blocking collectives, on_device(): lax.all_gather(partial_gain, 'seq')  26.9 us
    unnamed x31, local copies, waits for them, and re-layouts  20.3 us
    all_to_all x1, waiting for transfers between devices, on_device(): lax.all_to_all(back_cols, 'seq', split_axis=0, concat_axis=1, tiled=True)  17.7 us
    all_to_all x1, waiting for transfers between devices, on_device(): lax.all_to_all(grad_gate_cols, 'seq', split_axis=0, concat_axis=1, tiled=...  17.6 us
    unnamed x3, other arithmetic  16.3 us
    all_to_all x1, waiting for transfers between devices, on_device(): lax.all_to_all(first_mixed, 'seq', split_axis=1, concat_axis=0, tiled=True)  11 us
    all_to_all x1, waiting for transfers between devices, on_device(): lax.all_to_all(gates3, 'seq', split_axis=1, concat_axis=0, tiled=True)  11 us
    all_to_all x1, starting transfers between devices, on_device(): lax.all_to_all(first_mixed, 'seq', split_axis=1, concat_axis=0, tiled=True)  7.57 us
  transfers between devices with their start and end apart: 6, of which 5 were waited for; matrix products, arithmetic and copies ran while one was open for 20% of the time, Pallas kernels for 0%

profile of v1, /device:TPU:0, one launch (start us, length us, event | category | flops | bytes accessed | tf_op | source)
XLA Modules:
  0.0 184.7 jit_solution(15634811770722636075)
XLA Ops:
  0.6 0.0 copy-start
  0.6 1.1 copy-done
  1.8 1.6 fusion.5
  3.4 1.2 copy.83
  4.6 0.5 broadcast.2
  5.1 5.4 %reduce.3 = bf16[512,768]{1,0:T(8,128)(2,1)S(1)} reduce(bf16[512,1,768]{2,1,0:T(2,128)(2,1)S(1)} %bitcast.48, bf16[]{:T(256)} %broadcast.2), dimensions={1}, to_apply=%bitcast.46.reduce_sub_computation | reduce | bytes 1572866
  10.6 1.1 reshape.103
  11.6 0.0 copy-start.4
  11.6 7.6 %all-to-all-start.1 = ((bf16[16,2,12288]{2,1,0:T(2,128)(2,1)}), bf16[16,2,12288]{2,1,0:T(2,128)(2,1)}, u32[]{:S(2)}, u32[]{:S(2)}) async-start(bf16[16,2,12288]{2,1,0:T(2,128)(2,1)} %reshape.103), calls=%async_computation.1 | async-start | bytes 1572864 | tf_op jit(solution)/shard_map/all_to_all | solution.py:34
  19.2 0.0 copy-done.4
  19.2 1.2 copy.84
  20.4 5.4 %reduce.1 = bf16[512,768]{1,0:T(8,128)(2,1)S(1)} reduce(bf16[512,1,768]{2,1,0:T(2,128)(2,1)S(1)} %bitcast.53, bf16[]{:T(256)} %broadcast.2), dimensions={1}, to_apply=%bitcast.47.reduce_sub_computation | reduce | bytes 1572866
  25.9 1.1 reshape.105
  26.9 0.0 copy-start.5
  26.9 11.0 %all-to-all-done.1 = bf16[16,2,12288]{2,1,0:T(2,128)(2,1)} async-done(((bf16[16,2,12288]{2,1,0:T(2,128)(2,1)}), bf16[16,2,12288]{2,1,0:T(2,128)(2,1)}, u32[]{:S(2)}, u32[]{:S(2)}) %all-to-all-start.1) | async-done | bytes 786464 | tf_op jit(solution)/shard_map/all_to_all | solution.py:34
  38.0 5.5 %all-to-all-start = ((bf16[16,2,12288]{2,1,0:T(2,128)(2,1)}), bf16[16,2,12288]{2,1,0:T(2,128)(2,1)}, u32[]{:S(2)}, u32[]{:S(2)}) async-start(bf16[16,2,12288]{2,1,0:T(2,128)(2,1)} %reshape.105), calls=%async_computation | async-start | bytes 1572864 | tf_op jit(solution)/shard_map/all_to_all | solution.py:28
  43.5 0.0 copy-done.5
  43.5 1.2 copy.82
  44.7 5.4 %reduce.2 = bf16[512,768]{1,0:T(8,128)(2,1)S(1)} reduce(bf16[512,1,768]{2,1,0:T(2,128)(2,1)S(1)} %bitcast.49, bf16[]{:T(256)} %broadcast.2), dimensions={1}, to_apply=%bitcast.45.reduce_sub_computation | reduce | bytes 1572866
  50.2 0.0 copy-start.6
  50.2 1.1 reshape.107
  51.2 11.0 %all-to-all-done = bf16[16,2,12288]{2,1,0:T(2,128)(2,1)} async-done(((bf16[16,2,12288]{2,1,0:T(2,128)(2,1)}), bf16[16,2,12288]{2,1,0:T(2,128)(2,1)}, u32[]{:S(2)}, u32[]{:S(2)}) %all-to-all-start) | async-done | bytes 786464 | tf_op jit(solution)/shard_map/all_to_all | solution.py:28
  62.3 5.5 %all-to-all-start.3 = ((bf16[16,2,12288]{2,1,0:T(2,128)(2,1)}), bf16[16,2,12288]{2,1,0:T(2,128)(2,1)S(1)}, u32[]{:S(2)}, u32[]{:S(2)}) async-start(bf16[16,2,12288]{2,1,0:T(2,128)(2,1)} %reshape.107), calls=%async_computation.3 | async-start | bytes 1572864 | tf_op jit(solution)/shard_map/all_to_all | solution.py:29
  67.7 0.0 copy-done.6
  67.8 0.2 copy.46
  67.9 4.4 %reshape.104 = bf16[512,1,768]{2,1,0:T(2,128)(2,1)S(1)} reshape(bf16[16,2,12288]{2,1,0:T(2,128)(2,1)} %all-to-all-done.1) | data formatting | bytes 1572864
  72.3 1.0 copy.60
  73.3 4.4 %reshape.106 = bf16[512,1,768]{2,1,0:T(2,128)(2,1)S(1)} reshape(bf16[16,2,12288]{2,1,0:T(2,128)(2,1)} %all-to-all-done) | data formatting | bytes 1572864
  77.7 0.1 copy.43
  77.8 1.3 convert.3
  79.1 7.3 %all-to-all-done.3 = bf16[16,2,12288]{2,1,0:T(2,128)(2,1)S(1)} async-done(((bf16[16,2,12288]{2,1,0:T(2,128)(2,1)}), bf16[16,2,12288]{2,1,0:T(2,128)(2,1)S(1)}, u32[]{:S(2)}, u32[]{:S(2)}) %all-to-all-start.3) | async-done | bytes 786464 | tf_op jit(solution)/shard_map/all_to_all | solution.py:29
  86.4 0.7 reshape.108
  87.2 0.0 copy-start.7
  87.2 0.1 copy.50
  87.3 0.0 copy-start.1
  87.3 0.0 copy-start.2
  87.4 0.2 convert.4
  87.5 0.4 copy-done.7
  87.9 0.8 copy-done.1
  88.7 0.2 copy-done.2
  88.9 2.4 %fusion.2 = (f32[768]{0:T(1024)S(1)}, bf16[16,32,768]{2,0,1:T(8,128)(2,1)S(1)}, bf16[16,32,768]{2,0,1:T(8,128)(2,1)S(1)}, bf16[16,32,768]{2,0,1:T(8,128)(2,1)S(1)}) fusion(f32[16,32,768]{2,1,0:T(8,128)S(1)} %copy-done.1, f32[16,32,768]{2,1,0:T(8,128)S(1)} %convert.4, f32[768]{0:T(1024)S(1)} %copy-done.7, bf16[16,32,768]{2,1,0:T(8,128)(2,1)S(1)} %bitcast.58, ...), kind=kOutput, calls=%fused_computation.5 | convolution fusion | flops 17702144 | bytes 6314240 | tf_op jit(solution)/shard_map/jab,bjc->ajc/dot_general | solution.py:35
  91.4 0.0 copy-start.3
  91.4 0.9 copy-done.3
  92.3 0.4 fusion.4
  92.7 1.1 copy.54
  93.8 5.5 %all-to-all-start.4 = ((bf16[16,32,768]{2,1,0:T(8,128)(2,1)}), bf16[16,32,768]{2,1,0:T(8,128)(2,1)}, u32[]{:S(2)}, u32[]{:S(2)}) async-start(bf16[16,32,768]{2,1,0:T(8,128)(2,1)} %copy.54), calls=%async_computation.4 | async-start | bytes 1572864 | tf_op jit(solution)/shard_map/all_to_all | solution.py:55
  99.3 1.1 copy.56
  100.5 17.7 %all-to-all-done.4 = bf16[16,32,768]{2,1,0:T(8,128)(2,1)} async-done(((bf16[16,32,768]{2,1,0:T(8,128)(2,1)}), bf16[16,32,768]{2,1,0:T(8,128)(2,1)}, u32[]{:S(2)}, u32[]{:S(2)}) %all-to-all-start.4) | async-done | bytes 786464 | tf_op jit(solution)/shard_map/all_to_all | solution.py:55
  118.1 5.5 %all-to-all-start.5 = ((bf16[16,32,768]{2,1,0:T(8,128)(2,1)}), bf16[16,32,768]{2,1,0:T(8,128)(2,1)S(1)}, u32[]{:S(2)}, u32[]{:S(2)}) async-start(bf16[16,32,768]{2,1,0:T(8,128)(2,1)} %copy.56), calls=%async_computation.5 | async-start | bytes 1572864 | tf_op jit(solution)/shard_map/all_to_all | solution.py:57
  123.6 1.1 copy.48
  124.7 17.6 %all-to-all-done.5 = bf16[16,32,768]{2,1,0:T(8,128)(2,1)S(1)} async-done(((bf16[16,32,768]{2,1,0:T(8,128)(2,1)}), bf16[16,32,768]{2,1,0:T(8,128)(2,1)S(1)}, u32[]{:S(2)}, u32[]{:S(2)}) %all-to-all-start.5) | async-done | bytes 786464 | tf_op jit(solution)/shard_map/all_to_all | solution.py:57
  142.3 5.5 %all-to-all-start.2 = ((bf16[16,32,768]{2,1,0:T(8,128)(2,1)}), bf16[16,32,768]{2,1,0:T(8,128)(2,1)S(1)}, u32[]{:S(2)}, u32[]{:S(2)}) async-start(bf16[16,32,768]{2,1,0:T(8,128)(2,1)} %copy.48), calls=%async_computation.2 | async-start | bytes 1572864 | tf_op jit(solution)/shard_map/all_to_all | solution.py:56
  147.8 1.7 fusion.7
  149.5 0.0 copy-start.8
  149.5 0.8 copy.58
  150.3 26.9 %all-gather.1 = f32[16,1,768]{2,1,0:T(1,128)S(1)} all-gather(f32[1,1,768]{2,1,0:T(1,128)S(1)} %reshape.100), channel_id=2, replica_groups=mesh['groups'=2,'seq'=16] {'seq'}, dimensions={0}, use_global_device_ids=true | all-gather | bytes 52224 | tf_op jit(solution)/shard_map/all_gather | solution.py:59
  177.2 0.6 broadcast_multiply_fusion
  177.8 2.5 %fusion.6 = bf16[1,512,512]{2,1,0:T(8,128)(2,1)} fusion(bf16[512,768]{1,0:T(8,128)(2,1)} %bitcast.10, bf16[512,768]{1,0:T(8,128)(2,1)S(1)} %copy-done), kind=kOutput, calls=%fused_computation.16 | convolution fusion | flops 403439616 | bytes 2097152 | tf_op jit(solution)/shard_map/kac,kbc->kab/dot_general | solution.py:60
  180.4 0.0 copy-done.8
  180.4 2.6 %convolution_convert_fusion = bf16[512,768]{1,0:T(8,128)(2,1)} fusion(bf16[512,768]{1,0:T(8,128)(2,1)} %bitcast.10, bf16[1,512,512]{2,1,0:T(8,128)(2,1)S(1)} %copy-done.8), kind=kOutput, calls=%fused_computation.8 | convolution fusion | flops 403570688 | bytes 2097152 | tf_op jit(solution)/shard_map/kab,kac->kbc/dot_general | solution.py:66
  183.0 0.0 all-to-all-done.2
  183.0 0.9 copy.87
  183.9 0.9 copy.88
  (3 shorter events, 0.1 us)
Async XLA Ops:
  0.6 1.1 copy-start
  11.6 7.6 %copy-start.4 = (bf16[512,768]{1,0:T(8,128)(2,1)S(1)}, bf16[512,768]{1,0:T(8,128)(2,1)}, u32[]{:S(2)}) copy-start(bf16[512,768]{1,0:T(8,128)(2,1)} %param.7) | copy-start | bytes 2359300
  11.6 26.3 %all-to-all-start.1 = ((bf16[16,2,12288]{2,1,0:T(2,128)(2,1)}), bf16[16,2,12288]{2,1,0:T(2,128)(2,1)}, u32[]{:S(2)}, u32[]{:S(2)}) async-start(bf16[16,2,12288]{2,1,0:T(2,128)(2,1)} %reshape.103), calls=%async_computation.1 | async-start | bytes 1572864 | tf_op jit(solution)/shard_map/all_to_all | solution.py:34
  26.9 16.6 %copy-start.5 = (bf16[512,768]{1,0:T(8,128)(2,1)S(1)}, bf16[512,768]{1,0:T(8,128)(2,1)}, u32[]{:S(2)}) copy-start(bf16[512,768]{1,0:T(8,128)(2,1)} %param.8) | copy-start | bytes 2359300
  38.0 24.3 %all-to-all-start = ((bf16[16,2,12288]{2,1,0:T(2,128)(2,1)}), bf16[16,2,12288]{2,1,0:T(2,128)(2,1)}, u32[]{:S(2)}, u32[]{:S(2)}) async-start(bf16[16,2,12288]{2,1,0:T(2,128)(2,1)} %reshape.105), calls=%async_computation | async-start | bytes 1572864 | tf_op jit(solution)/shard_map/all_to_all | solution.py:28
  50.2 17.6 %copy-start.6 = (bf16[32,16,16]{0,2,1:T(8,128)(2,1)S(1)}, bf16[32,16,16]{0,2,1:T(8,128)(2,1)}, u32[]{:S(2)}) copy-start(bf16[32,16,16]{0,2,1:T(8,128)(2,1)} %param.10) | copy-start | bytes 49156
  62.3 24.2 %all-to-all-start.3 = ((bf16[16,2,12288]{2,1,0:T(2,128)(2,1)}), bf16[16,2,12288]{2,1,0:T(2,128)(2,1)S(1)}, u32[]{:S(2)}, u32[]{:S(2)}) async-start(bf16[16,2,12288]{2,1,0:T(2,128)(2,1)} %reshape.107), calls=%async_computation.3 | async-start | bytes 1572864 | tf_op jit(solution)/shard_map/all_to_all | solution.py:29
  87.2 0.7 copy-start.7
  87.3 1.4 copy-start.1
  87.3 1.6 copy-start.2
  91.4 0.9 copy-start.3
  93.8 24.3 %all-to-all-start.4 = ((bf16[16,32,768]{2,1,0:T(8,128)(2,1)}), bf16[16,32,768]{2,1,0:T(8,128)(2,1)}, u32[]{:S(2)}, u32[]{:S(2)}) async-start(bf16[16,32,768]{2,1,0:T(8,128)(2,1)} %copy.54), calls=%async_computation.4 | async-start | bytes 1572864 | tf_op jit(solution)/shard_map/all_to_all | solution.py:55
  118.1 24.2 %all-to-all-start.5 = ((bf16[16,32,768]{2,1,0:T(8,128)(2,1)}), bf16[16,32,768]{2,1,0:T(8,128)(2,1)S(1)}, u32[]{:S(2)}, u32[]{:S(2)}) async-start(bf16[16,32,768]{2,1,0:T(8,128)(2,1)} %copy.56), calls=%async_computation.5 | async-start | bytes 1572864 | tf_op jit(solution)/shard_map/all_to_all | solution.py:57
  142.3 40.7 %all-to-all-start.2 = ((bf16[16,32,768]{2,1,0:T(8,128)(2,1)}), bf16[16,32,768]{2,1,0:T(8,128)(2,1)S(1)}, u32[]{:S(2)}, u32[]{:S(2)}) async-start(bf16[16,32,768]{2,1,0:T(8,128)(2,1)} %copy.48), calls=%async_computation.2 | async-start | bytes 1572864 | tf_op jit(solution)/shard_map/all_to_all | solution.py:56
  149.5 30.9 %copy-start.8 = (bf16[1,512,512]{2,1,0:T(8,128)(2,1)S(1)}, bf16[1,512,512]{2,1,0:T(8,128)(2,1)}, u32[]{:S(2)}) copy-start(bf16[1,512,512]{2,1,0:T(8,128)(2,1)} %param.9) | copy-start | bytes 1572868
